TPU v7x, 128 devices: a whole 4x4x4 slice. The times are simulated.
128 devices in a mesh: rep: 4 (over y), row: 32 (over x, z, core).
Axes of the slice: x: 4, y: 4, z: 4, core: 2. Of those that a mesh axis runs over, the one named last changes fastest.
Arguments:
- grads: bfloat16 [4, 2, 6144, 8192], P('rep', None, 'row'), may hold values from -6 to 6
- errors: bfloat16 [4, 2, 6144, 8192], P('rep', None, 'row'), may hold values from -4 to 4
- q_init: float32 [2, 32, 8192], replicated, may hold values from -0.0625 to 0.0625
Outputs:
- new_errors: bfloat16 [4, 2, 6144, 8192], P('rep', None, 'row')
- q_new: float32 [2, 32, 8192], replicated
All inputs are finite; a program needn't handle non-finite values.
Results may differ from a plain program's by a relative error of at most 0.001.
Values sent between devices are 32-bit elements; how exact they have to be, the bound alone decides.
A program may use at most 128 MiB of HBM per device.

v0:
```python
import jax
import jax.numpy as jnp
from jax import lax
from jax.sharding import PartitionSpec as P


def compress(merged, q_start):
    high = lax.Precision.HIGHEST
    replicas = lax.axis_size("rep")
    local_panel = jnp.einsum("erf,ekf->erk", merged, q_start, precision=high)
    panel = lax.psum(local_panel, "rep") / replicas
    gram_part = jnp.einsum("erk,erl->ekl", panel, panel, precision=high)
    gram_total = lax.psum(gram_part, "row")
    factor = jnp.linalg.cholesky(gram_total)
    identity = jnp.broadcast_to(jnp.eye(factor.shape[-1], dtype=jnp.float32), factor.shape)
    inverse = lax.linalg.triangular_solve(factor, identity, left_side=True, lower=True)
    basis = jnp.einsum("erk,elk->erl", panel, inverse, precision=high)
    coeff_part = jnp.einsum("erf,erk->ekf", merged, basis, precision=high)
    coeffs = lax.psum(coeff_part, ("rep", "row")) / replicas
    fresh = (merged - jnp.einsum("erk,ekf->erf", basis, coeffs, precision=high)).astype(
        jnp.bfloat16
    )
    return (fresh, coeffs)


def shards(grads, errors, q_init):
    merged = grads[0].astype(jnp.float32) + errors[0].astype(jnp.float32)
    fresh_list = []
    coeff_list = []
    for expert in range(merged.shape[0]):
        one_fresh, one_coeffs = compress(merged[expert : expert + 1], q_init[expert : expert + 1])
        fresh_list.append(one_fresh)
        coeff_list.append(one_coeffs)
    fresh = jnp.concatenate(fresh_list, axis=0)
    coeffs = jnp.concatenate(coeff_list, axis=0)
    return (fresh[None], coeffs)


def solution(mesh):
    in_specs = (P("rep", None, "row", None), P("rep", None, "row", None), P())
    out_specs = (P("rep", None, "row", None), P())
    return jax.shard_map(shards, mesh=mesh, in_specs=in_specs, out_specs=out_specs, check_vma=False)
```

profile of v0, /device:TPU:1, one launch (start us, length us, event | category | flops | bytes accessed | tf_op | source)
XLA Modules:
  0.0 381.2 jit_solution(12928234375953716499)
XLA Ops:
  7.2 0.0 all-reduce.5.cloned.1.call-start
  7.2 11.7 %convert_add_fusion = f32[1,2,192,8192]{3,2,1,0:T(8,128)} fusion(bf16[1,2,192,8192]{3,2,1,0:T(8,128)(2,1)} %param.7, bf16[1,2,192,8192]{3,2,1,0:T(8,128)(2,1)} %param.6), kind=kLoop, calls=%fused_computation | loop fusion | flops 9437184 | bytes 25165824 | tf_op jit(solution)/shard_map/add | solution.py:27
  18.9 7.7 %fusion.17 = f32[1,192,32]{1,2,0:T(8,128)S(1)} fusion(f32[1,2,192,8192]{3,2,1,0:T(8,128)} %convert_add_fusion, f32[2,32,8192]{2,1,0:T(8,128)S(1)} %copy-done.2), kind=kOutput, calls=%fused_computation.22 | convolution fusion | flops 603979776 | bytes 7364608 | tf_op jit(solution)/shard_map/erf,ekf->erk/dot_general | solution.py:10
  26.6 7.7 %fusion.14 = f32[1,192,32]{1,2,0:T(8,128)S(1)} fusion(f32[1,2,192,8192]{3,2,1,0:T(8,128)} %convert_add_fusion, f32[2,32,8192]{2,1,0:T(8,128)S(1)} %copy-done.2), kind=kOutput, calls=%fused_computation.21 | convolution fusion | flops 603979776 | bytes 7364608 | tf_op jit(solution)/shard_map/erf,ekf->erk/dot_general | solution.py:10
  34.3 14.9 %all-reduce.2 = (f32[1,192,32]{1,2,0:T(8,128)S(1)}, f32[1,192,32]{1,2,0:T(8,128)S(1)}) all-reduce(f32[1,192,32]{1,2,0:T(8,128)S(1)} %fusion.17, f32[1,192,32]{1,2,0:T(8,128)S(1)} %fusion.14), channel_id=1, replica_groups=mesh['rep'=4,'row'=32] {'rep'}, use_global_device_ids=true, to_apply=%region_5.8 | all-reduce | flops 12288 | bytes 98304 | tf_op jit(solution)/shard_map/psum | solution.py:11
  49.2 0.2 convolution_bitcast_fusion.4
  49.3 0.2 convolution_bitcast_fusion.5
  49.5 124.6 %all-reduce.1 = (f32[1,32,32]{1,2,0:T(8,128)S(1)}, f32[1,32,32]{1,2,0:T(8,128)S(1)}) all-reduce(f32[1,32,32]{1,2,0:T(8,128)S(1)} %convolution_bitcast_fusion.4, f32[1,32,32]{1,2,0:T(8,128)S(1)} %convolution_bitcast_fusion.5), channel_id=1, replica_groups=mesh['rep'=4,'row'=32] {'row'}, use_global_device_ids=true, to_apply=%region_6.9 | all-reduce | flops 2048 | bytes 16384 | tf_op jit(solution)/shard_map/psum | solution.py:13
  174.1 0.1 copy.8
  174.2 0.1 copy.6
  174.3 2.9 custom-call.10
  177.2 0.6 compare_reduce_fusion
  177.9 0.7 fusion.37
  178.5 2.4 custom-call.11
  181.0 0.2 fusion.38
  181.2 0.2 fusion.26
  181.4 7.6 %convolution_bitcast_fusion.2 = f32[1,32,8192]{2,1,0:T(8,128)} fusion(f32[192,32]{0,1:T(8,128)S(1)} %fusion.26, f32[1,2,192,8192]{3,2,1,0:T(8,128)} %convert_add_fusion), kind=kOutput, calls=%fused_computation.7 | convolution fusion | flops 603979776 | bytes 7364608 | tf_op jit(solution)/shard_map/erf,erk->ekf/dot_general | solution.py:18
  189.0 2.9 custom-call.8
  192.0 0.6 compare_reduce_fusion.1
  192.6 0.7 fusion.36
  193.3 2.4 custom-call.9
  195.7 0.2 fusion.42
  195.9 0.2 fusion.29
  196.1 7.6 %convolution_bitcast_fusion.3 = f32[1,32,8192]{2,1,0:T(8,128)} fusion(f32[192,32]{0,1:T(8,128)S(1)} %fusion.29, f32[1,2,192,8192]{3,2,1,0:T(8,128)} %convert_add_fusion), kind=kOutput, calls=%fused_computation.8 | convolution fusion | flops 603979776 | bytes 7364608 | tf_op jit(solution)/shard_map/erf,erk->ekf/dot_general | solution.py:18
  203.7 0.0 all-reduce.5.cloned.1.call-update
  203.8 150.4 %all-reduce.5.cloned.1.call-done = (f32[1,32,8192]{2,1,0:T(8,128)}, f32[1,32,8192]{2,1,0:T(8,128)}) async-done(((f32[1,32,8192]{2,1,0:T(8,128)}, f32[1,32,8192]{2,1,0:T(8,128)}), (f32[1,32,8192]{2,1,0:T(8,128)}, f32[1,32,8192]{2,1,0:T(8,128)})) %all-reduce.5.cloned.1.call-update) | async-done | bytes 2097168 | tf_op jit(solution)/shard_map/psum | solution.py:19
  354.2 7.7 %fusion.2 = bf16[1,192,8192]{2,1,0:T(8,128)(2,1)S(1)} fusion(f32[192,32]{0,1:T(8,128)S(1)} %fusion.26, f32[1,2,192,8192]{3,2,1,0:T(8,128)} %convert_add_fusion, f32[1,32,8192]{2,1,0:T(8,128)} %get-tuple-element.4), kind=kOutput, calls=%fused_computation.5 | convolution fusion | flops 607387648 | bytes 10510336 | tf_op jit(solution)/shard_map/erk,ekf->erf/dot_general | solution.py:20
  361.9 0.1 broadcast_multiply_fusion
  362.0 7.6 %fusion.3 = bf16[1,192,8192]{2,1,0:T(8,128)(2,1)S(1)} fusion(f32[192,32]{0,1:T(8,128)S(1)} %fusion.29, f32[1,2,192,8192]{3,2,1,0:T(8,128)} %convert_add_fusion, f32[1,32,8192]{2,1,0:T(8,128)S(1)} %copy-done), kind=kOutput, calls=%fused_computation.6 | convolution fusion | flops 607387648 | bytes 10510336 | tf_op jit(solution)/shard_map/erk,ekf->erf/dot_general | solution.py:20
  369.6 0.1 broadcast_multiply_fusion.1
  369.6 3.2 maximum_bitcast_fusion
  372.9 1.5 pad_maximum_fusion
  (9 shorter events, 0.1 us)
Async XLA Ops:
  7.2 11.8 %copy-start.2 = (f32[2,32,8192]{2,1,0:T(8,128)S(1)}, f32[2,32,8192]{2,1,0:T(8,128)}, u32[]{:S(2)}) copy-start(f32[2,32,8192]{2,1,0:T(8,128)} %param.8) | copy-start | bytes 6291460
  7.2 347.0 %all-reduce.5.cloned.1.call-start = ((), (), s32[]{:S(2)}) async-start(), calls=%async_computation | async-start | bytes 4194304 | tf_op jit(solution)/shard_map/psum | solution.py:19
  354.2 7.7 %copy-start.1 = (f32[1,32,8192]{2,1,0:T(8,128)S(1)}, f32[1,32,8192]{2,1,0:T(8,128)}, u32[]{:S(2)}) copy-start(f32[1,32,8192]{2,1,0:T(8,128)} %get-tuple-element.4) | copy-start | bytes 3145732
  354.2 7.8 %copy-start = (f32[1,32,8192]{2,1,0:T(8,128)S(1)}, f32[1,32,8192]{2,1,0:T(8,128)}, u32[]{:S(2)}) copy-start(f32[1,32,8192]{2,1,0:T(8,128)} %get-tuple-element.5) | copy-start | bytes 3145732
Sparse Core Ops, SparseCore 0:
  203.9 150.2 all-reduce.4
where the time goes:
time: 381 us
  waiting for transfers between devices  150 us (39%)
  blocking collectives  140 us (37%)
  matrix products  47 us (12%)
  other arithmetic  29.9 us (8%)
  between operations  14.2 us (4%)
    psum x1, waiting for transfers between devices, compress(): coeffs = lax.psum(coeff_part, ('rep', 'row')) / replicas  150 us
    psum x1, blocking collectives, compress(): gram_total = lax.psum(gram_part, 'row')  125 us
    dot_general x2, matrix products, compress(): local_panel = jnp.einsum('erf,ekf->erk', merged, q_start, precision=high)  15.3 us
    dot_general x2, matrix products, compress(): jnp.einsum('erk,ekf->erf', basis, coeffs, precision=high)  15.3 us
    dot_general x2, matrix products, compress(): coeff_part = jnp.einsum('erf,erk->ekf', merged, basis, precision=high)  15.3 us
    psum x1, blocking collectives, compress(): panel = lax.psum(local_panel, 'rep') / replicas  14.9 us
    add x1, other arithmetic, shards(): merged = grads[0].astype(jnp.float32) + errors[0].astype(jnp.float32)  11.7 us
  transfers between devices with their start and end apart: 1, of which 1 were waited for; matrix products, arithmetic and copies ran while one was open for 0% of the time, Pallas kernels for 0%

commit v1 on v0

v1 whole, which is shorter than its diff:
```python
import jax
import jax.numpy as jnp
from jax import lax
from jax.experimental import pallas as pl
from jax.experimental.pallas import tpu as pltpu
from jax.sharding import PartitionSpec as P

EXP, ROWS, FF, R = 2, 192, 8192, 32
REPS, SIDE = 4, 4
UNITS = 4
UNIT = FF // UNITS
PIECE = UNIT // SIDE
TILE = PIECE // SIDE
MESH = pl.DeviceIdType.MESH
HIGH = lax.Precision.HIGHEST
NN = (((1,), (0,)), ((), ()))
NT = (((1,), (1,)), ((), ()))


def split(value, pieces):
    out = []
    for _ in range(pieces):
        piece = value.astype(jnp.bfloat16)
        out.append(piece)
        value = value - piece.astype(jnp.float32)
    return out


def dot(a, b, dims=NN):
    return lax.dot_general(a, b, dims, preferred_element_type=jnp.float32)


def dot_high(a, b, dims=NN):
    return lax.dot_general(a, b, dims, precision=HIGH, preferred_element_type=jnp.float32)


def kernel(
    g_hbm, e_hbm, q_hbm, fresh, coeffs,
    g, e, q, panels, left, basis, gram1, gram2, aug_ref, part, partner, r1, s2, r2, t3, full,
    load_sem, ps, pr, g1s, g1r, g2s, g2r, cs, cr, s1s, s1r, s2s, s2r, s3s, s3r, a2s, a2r, a1s, a1r, fs, fr,
):
    y = lax.axis_index("rep")
    row = lax.axis_index("row")
    c = lax.rem(row, 2)
    z = lax.rem(row // 2, SIDE)
    x = row // (2 * SIDE)
    me = (x, y, z)

    def at(place, core):
        return (place[1], place[0] * (2 * SIDE) + place[2] * 2 + core)

    def along(axis, d):
        return at([lax.rem(p + d * w, SIDE) for p, w in zip(me, axis)], c)

    def my(axis):
        return x * axis[0] + y * axis[1] + z * axis[2]

    ax, ay, az = (1, 0, 0), (0, 1, 0), (0, 0, 1)
    n = 1 - c
    orders = [(ax, ay, az), (ay, az, ax), (az, ax, ay), ((n, c, 0), (0, n, c), (c, 0, n))]
    other = at(me, 1 - c)

    def remote(src, dst, send, recv, device):
        return pltpu.make_async_remote_copy(
            src_ref=src, dst_ref=dst, send_sem=send, recv_sem=recv, device_id=device, device_id_type=MESH
        )

    loads = []
    for ex in range(EXP):
        for u in range(UNITS):
            cols = pl.ds(u * UNIT, UNIT)
            group = [
                pltpu.make_async_copy(q_hbm.at[ex, :, cols], q.at[ex, :, cols], load_sem.at[0, ex, u]),
                pltpu.make_async_copy(g_hbm.at[0, ex, :, cols], g.at[ex, :, cols], load_sem.at[1, ex, u]),
                pltpu.make_async_copy(e_hbm.at[0, ex, :, cols], e.at[ex, :, cols], load_sem.at[2, ex, u]),
            ]
            for copy in group:
                copy.start()
            loads.append(group)

    barrier = pltpu.get_barrier_semaphore()
    greeted = [along(axis, d) for axis in (ax, ay, az) for d in (1, 2, 3)]
    greeted += [at((lax.rem(x + d, SIDE), y, z), 1 - c) for d in range(SIDE)]
    for device in greeted:
        pl.semaphore_signal(barrier, inc=1, device_id=device, device_id_type=MESH)

    sends = []
    panel_recvs = []
    for ex in range(EXP):
        total = jnp.zeros((ROWS, 3 * R), jnp.float32)
        for u in range(UNITS):
            for copy in loads[ex * UNITS + u]:
                copy.wait()
            cols = pl.ds(u * UNIT, UNIT)
            q3 = jnp.concatenate(split(q[ex, :, cols], 3), axis=0)
            total += dot(g[ex, :, cols], q3, NT)
            total += dot(e[ex, :, cols], q3, NT)
        flat = jnp.concatenate([total, jnp.zeros((ROWS, R), jnp.float32)], axis=1).T
        panels[ex, y] = flat[0:R] + flat[R : 2 * R] + flat[2 * R : 3 * R]
        if ex == 0:
            pl.semaphore_wait(barrier, len(greeted))
        recvs = []
        for d in (1, 2, 3):
            copy = remote(panels.at[ex, y], panels.at[ex, y], ps.at[ex, d - 1], pr.at[ex, d - 1], along(ay, d))
            copy.start()
            sends.append(copy)
            recvs.append(copy)
        panel_recvs.append(recvs)

    def finish_panel(ex):
        for copy in panel_recvs[ex]:
            copy.wait_recv()
        panel = (panels[ex, 0] + panels[ex, 1] + panels[ex, 2] + panels[ex, 3]) * (1.0 / REPS)
        left[ex] = jnp.concatenate(split(panel, 3), axis=0)
        return panel

    def product(ex, u):
        def body(p, _):
            cols = pl.ds(pl.multiple_of(u * UNIT + p * PIECE, PIECE), PIECE)
            lhs = left[ex]
            both = dot(lhs, g[ex, :, cols]) + dot(lhs, e[ex, :, cols])
            part[ex, u, p] = both[0:R] + both[R : 2 * R] + both[2 * R : 3 * R]
            return 0

        lax.fori_loop(0, SIDE, body, 0)

    def to_partner(ex, u):
        return remote(part.at[ex, u], partner.at[u], cs.at[u], cr.at[u], other)

    def scatter1(ex, u, d):
        axis = orders[u][0]
        p = lax.rem(my(axis) + d, SIDE)
        return remote(part.at[ex, u, p], r1.at[u, d - 1], s1s.at[u, d - 1], s1r.at[u, d - 1], along(axis, d))

    def own_unit(ex, u):
        to_partner(ex, u).wait_recv()
        for p in range(SIDE):
            part[ex, u, p] = part[ex, u, p] + partner[u, p]
        for d in (1, 2, 3):
            scatter1(ex, u, d).start()

    def coefficients(ex):
        for u in range(UNITS):
            product(ex, u)

            @pl.when(c != ex)
            def _():
                to_partner(ex, u).start()

            if u > 0:

                @pl.when(c == ex)
                def _():
                    own_unit(ex, u - 1)

        @pl.when(c == ex)
        def _():
            own_unit(ex, UNITS - 1)

    panel0 = finish_panel(0)
    coefficients(0)
    panel1 = finish_panel(1)

    zeros = jnp.zeros((R, ROWS), jnp.float32)
    pad0 = jnp.concatenate([panel0, zeros, zeros, zeros], axis=0)
    pad1 = jnp.concatenate([zeros, zeros, panel1, zeros], axis=0)
    gram1[2 * x + c] = dot_high(panel0, pad0, NT) + dot_high(panel1, pad1, NT)
    gram1_copies = []
    for i in range(7):
        if i < 3:
            device = along(ax, i + 1)
        else:
            device = at((lax.rem(x + i - 3, SIDE), y, z), 1 - c)
        copy = remote(gram1.at[2 * x + c], gram1.at[2 * x + c], g1s.at[i], g1r.at[i], device)
        copy.start()
        gram1_copies.append(copy)

    coefficients(1)

    for copy in gram1_copies:
        copy.wait_recv()
    total = gram1[0]
    for i in range(1, 2 * SIDE):
        total += gram1[i]
    gram2[z] = total
    gram2_copies = []
    for d in (1, 2, 3):
        copy = remote(gram2.at[z], gram2.at[z], g2s.at[d - 1], g2r.at[d - 1], along(az, d))
        copy.start()
        gram2_copies.append(copy)

    def scatter2(u, d):
        axis = orders[u][1]
        p = lax.rem(my(axis) + d, SIDE)
        return remote(s2.at[u, p], r2.at[u, d - 1], s2s.at[u, d - 1], s2r.at[u, d - 1], along(axis, d))

    def scatter3(u, d):
        axis = orders[u][2]
        i = my(axis)
        return remote(t3.at[u, i], t3.at[u, i], s3s.at[u, d - 1], s3r.at[u, d - 1], along(axis, d))

    for u in range(UNITS):
        for d in (1, 2, 3):
            scatter1(c, u, d).wait_recv()
        mine = part[c, u, my(orders[u][0])] + r1[u, 0] + r1[u, 1] + r1[u, 2]
        for p in range(SIDE):
            s2[u, p] = mine[:, p * TILE : (p + 1) * TILE]
        for d in (1, 2, 3):
            scatter2(u, d).start()

    for copy in gram2_copies:
        copy.wait_recv()
    aug = gram2[0] + gram2[1] + gram2[2] + gram2[3]
    rows_at = lax.broadcasted_iota(jnp.int32, (R, 4 * R), 0)
    lanes_at = lax.broadcasted_iota(jnp.int32, (R, 4 * R), 1)
    unit_at = (lanes_at == rows_at + R) | (lanes_at == rows_at + 3 * R)
    aug = jnp.where(unit_at, 1.0, aug)
    first = lanes_at < 2 * R
    pivots = jnp.ones((R, 4 * R), jnp.float32)
    for k in range(R):
        column = jnp.where(first, aug[:, k : k + 1], aug[:, 2 * R + k : 2 * R + k + 1])
        pivot = column[k : k + 1, :]
        ratio = aug[k : k + 1, :] / pivot
        pivots = jnp.where(rows_at == k, pivot, pivots)
        aug = jnp.where(rows_at > k, aug - column * ratio, aug)
    aug = aug / jnp.sqrt(pivots)
    inverses = []
    for ex in range(EXP):
        wanted = (lanes_at >= (2 * ex + 1) * R) & (lanes_at < (2 * ex + 2) * R)
        inverses.append(jnp.where(wanted, aug, 0.0))
    aug_ref[0] = inverses[0]
    aug_ref[1] = inverses[1]

    for u in range(UNITS):
        for d in (1, 2, 3):
            scatter2(u, d).wait_recv()
        t3[u, my(orders[u][2])] = s2[u, my(orders[u][1])] + r2[u, 0] + r2[u, 1] + r2[u, 2]
        for d in (1, 2, 3):
            scatter3(u, d).start()

    for ex, panel in ((0, panel0), (1, panel1)):
        b = dot_high(inverses[ex], jnp.concatenate([panel] * 4, axis=0))
        hi, lo = [piece.astype(jnp.float32) for piece in split(b, 2)]
        basis[ex] = jnp.concatenate([hi, hi, lo, lo], axis=0).T.astype(jnp.bfloat16)

    def place(u):
        return c, u, my(orders[u][0]), my(orders[u][1])

    def gather2(u, d):
        spot = full.at[place(u)]
        return remote(spot, spot, a2s.at[u, d - 1], a2r.at[u, d - 1], along(orders[u][1], d))

    def gather1(u, d):
        spot = full.at[c, u, my(orders[u][0])]
        return remote(spot, spot, a1s.at[u, d - 1], a1r.at[u, d - 1], along(orders[u][0], d))

    def forward(u):
        return remote(full.at[c, u], full.at[c, u], fs.at[u], fr.at[u], other)

    for u in range(UNITS):
        for d in (1, 2, 3):
            scatter3(u, d).wait_recv()
        tile = t3[u, 0] + t3[u, 1] + t3[u, 2] + t3[u, 3]
        full[place(u)] = dot_high(aug_ref[c], jnp.concatenate([tile] * 4, axis=0)) * (1.0 / REPS)
        for d in (1, 2, 3):
            gather2(u, d).start()
    for u in range(UNITS):
        for d in (1, 2, 3):
            gather2(u, d).wait_recv()
        for d in (1, 2, 3):
            gather1(u, d).start()

    def residual(ex, u):
        def body(p, _):
            cols = pl.ds(pl.multiple_of(u * UNIT + p * PIECE, PIECE), PIECE)
            new = jnp.concatenate([full[ex, u, p, i] for i in range(SIDE)], axis=1)
            coeffs[ex, :, cols] = new
            hi, lo = split(new, 2)
            low = dot(basis[ex], jnp.concatenate([hi, lo, hi, lo], axis=0))
            merged = g[ex, :, cols].astype(jnp.float32) + e[ex, :, cols].astype(jnp.float32)
            fresh[0, ex, :, cols] = (merged - low).astype(jnp.bfloat16)
            return 0

        lax.fori_loop(0, SIDE, body, 0)

    for u in range(UNITS):
        for d in (1, 2, 3):
            gather1(u, d).wait_recv()
        forward(u).start()
        residual(c, u)
    for u in range(UNITS):
        forward(u).wait_recv()
        residual(1 - c, u)

    for copy in sends + gram1_copies + gram2_copies:
        copy.wait_send()
    for u in range(UNITS):
        to_partner(1 - c, u).wait_send()
        forward(u).wait_send()
        for d in (1, 2, 3):
            for copy in (scatter1(c, u, d), scatter2(u, d), scatter3(u, d), gather2(u, d), gather1(u, d)):
                copy.wait_send()


def shards(grads, errors, q_init):
    dma = pltpu.SemaphoreType.DMA
    anywhere = pl.BlockSpec(memory_space=pl.ANY)
    vmem = pl.BlockSpec(memory_space=pltpu.VMEM)
    f32, b16 = jnp.float32, jnp.bfloat16
    return pl.pallas_call(
        kernel,
        out_shape=(
            jax.ShapeDtypeStruct((1, EXP, ROWS, FF), b16),
            jax.ShapeDtypeStruct((EXP, R, FF), f32),
        ),
        in_specs=[anywhere] * 3,
        out_specs=(vmem, vmem),
        scratch_shapes=[
            pltpu.VMEM((EXP, ROWS, FF), b16),
            pltpu.VMEM((EXP, ROWS, FF), b16),
            pltpu.VMEM((EXP, R, FF), f32),
            pltpu.VMEM((EXP, REPS, R, ROWS), f32),
            pltpu.VMEM((EXP, 3 * R, ROWS), b16),
            pltpu.VMEM((EXP, ROWS, 4 * R), b16),
            pltpu.VMEM((2 * SIDE, R, 4 * R), f32),
            pltpu.VMEM((SIDE, R, 4 * R), f32),
            pltpu.VMEM((EXP, R, 4 * R), f32),
            pltpu.VMEM((EXP, UNITS, SIDE, R, PIECE), f32),
            pltpu.VMEM((UNITS, SIDE, R, PIECE), f32),
            pltpu.VMEM((UNITS, SIDE - 1, R, PIECE), f32),
            pltpu.VMEM((UNITS, SIDE, R, TILE), f32),
            pltpu.VMEM((UNITS, SIDE - 1, R, TILE), f32),
            pltpu.VMEM((UNITS, SIDE, R, TILE), f32),
            pltpu.VMEM((EXP, UNITS, SIDE, SIDE, R, TILE), f32),
            dma((3, EXP, UNITS)),
            dma((EXP, 3)), dma((EXP, 3)),
            dma((7,)), dma((7,)), dma((3,)), dma((3,)),
            dma((UNITS,)), dma((UNITS,)),
            dma((UNITS, 3)), dma((UNITS, 3)),
            dma((UNITS, 3)), dma((UNITS, 3)),
            dma((UNITS, 3)), dma((UNITS, 3)),
            dma((UNITS, 3)), dma((UNITS, 3)),
            dma((UNITS, 3)), dma((UNITS, 3)),
            dma((UNITS,)), dma((UNITS,)),
        ],
        compiler_params=pltpu.CompilerParams(
            collective_id=0, has_side_effects=True, vmem_limit_bytes=56 * 2**20
        ),
        cost_estimate=pl.CostEstimate(flops=10**9, bytes_accessed=25 * 10**6, transcendentals=0),
        name="compress",
    )(grads, errors, q_init)


def solution(mesh):
    in_specs = (P("rep", None, "row", None), P("rep", None, "row", None), P())
    out_specs = (P("rep", None, "row", None), P())
    return jax.shard_map(shards, mesh=mesh, in_specs=in_specs, out_specs=out_specs, check_vma=False)
```

time: 381 us -> 62.6 us (0.16)
  waiting for transfers between devices: 150 us -> 0 us
  blocking collectives: 140 us -> 0 us
  Pallas kernels: 0 us -> 54.2 us
  matrix products: 47 us -> 0 us
  other arithmetic: 29.9 us -> 0 us
  between operations: 14.2 us -> 0.65 us
  local copies, waits for them, and re-layouts: 0.15 us -> 7.67 us
    psum x1 -> x0, waiting for transfers between devices: 150 us -> none  [compress(): coeffs = lax.psum(coeff_part, ('rep', 'row')) / replicas]
    psum x2 -> x0, blocking collectives: 140 us -> none  [the longest x1 125 us: compress(): gram_total = lax.psum(gram_part, 'row')]
    pallas_call x0 -> x1, Pallas kernels: none -> 54.2 us  [shards(): pl.pallas_call(kernel, out_shape=(jax.ShapeDtypeStruct((1, EXP, ROWS, FF)...]
    dot_general x10 -> x0, matrix products: 46.5 us -> none  [the longest x2 15.3 us: compress(): local_panel = jnp.einsum('erf,ekf->erk', merged, q_start, precision=high)]
    another operation x10 -> x0, other arithmetic: 13.3 us -> none  [the longest x6 7.18 us: compress(): factor = jnp.linalg.cholesky(gram_total)]
    add x1 -> x0, other arithmetic: 11.7 us -> none  [shards(): merged = grads[0].astype(jnp.float32) + errors[0].astype(jnp.float32)]
    unnamed x6 -> x4, local copies, waits for them, and re-layouts: 0.01 us -> 7.67 us
  transfers between devices with their start and end apart: 1 -> 0, of which waited for: 1 -> 0; matrix products, arithmetic and copies ran while one was open for 0% -> 0% of each run, Pallas kernels for 0% -> 0%
where the time goes in v1:
time: 62.6 us; the launch traced here: 62.5 us
  Pallas kernels  54.2 us (87%)
  local copies, waits for them, and re-layouts  7.67 us (12%)
  between operations  0.65 us (1%)
    pallas_call x1, Pallas kernels, shards(): pl.pallas_call(kernel, out_shape=(jax.ShapeDtypeStruct((1, EXP, ROWS, FF)...  54.2 us
    unnamed x4, local copies, waits for them, and re-layouts  7.67 us

profile of v1, /device:TPU:1, one launch (start us, length us, event | category | flops | bytes accessed | tf_op | source)
XLA Modules:
  0.0 62.5 jit_solution(8478345646067023599)
XLA Ops:
  0.6 54.2 %compress.1 = (bf16[1,2,192,8192]{3,2,1,0:T(8,128)(2,1)}, f32[2,32,8192]{2,1,0:T(8,128)}) custom-call(bf16[1,2,192,8192]{3,2,1,0:T(8,128)(2,1)} %g_hbm.1, bf16[1,2,192,8192]{3,2,1,0:T(8,128)(2,1)} %e_hbm.1, f32[2,32,8192]{2,1,0:T(8,128)} %q_hbm.1), custom_call_target="tpu_custom_call" | custom-call | flops 1000000000 | bytes 25000000 | tf_op jit(solution)/shard_map/compress/pallas_call | solution.py:310
  54.8 0.0 copy-start
  54.8 6.3 %copy.7 = bf16[1,2,192,8192]{3,2,1,0:T(8,128)(2,1)} copy(bf16[1,2,192,8192]{3,2,1,0:T(8,128)(2,1)} %get-tuple-element.4) | data formatting | bytes 12582912
  61.1 0.0 copy-done
  61.2 1.3 %copy.8 = f32[2,32,8192]{2,1,0:T(8,128)} copy(f32[2,32,8192]{2,1,0:T(8,128)S(1)} %copy-done) | data formatting | bytes 4194304
Async XLA Ops:
  54.8 6.4 %copy-start = (f32[2,32,8192]{2,1,0:T(8,128)S(1)}, f32[2,32,8192]{2,1,0:T(8,128)}, u32[]{:S(2)}) copy-start(f32[2,32,8192]{2,1,0:T(8,128)} %get-tuple-element.5) | copy-start | bytes 6291460

commit v2 on v1

--- a/solution.py
+++ b/solution.py
@@ -11,6 +11,9 @@
 UNIT = FF // UNITS
 PIECE = UNIT // SIDE
 TILE = PIECE // SIDE
+LANES = 128
+LOADS = 2
+LOAD = FF // LOADS
 MESH = pl.DeviceIdType.MESH
 HIGH = lax.Precision.HIGHEST
 NN = (((1,), (0,)), ((), ()))
@@ -65,18 +68,18 @@
             src_ref=src, dst_ref=dst, send_sem=send, recv_sem=recv, device_id=device, device_id_type=MESH
         )
 
-    loads = []
+    def loads(ex, h):
+        cols = pl.ds(pl.multiple_of(h * LOAD, LOAD), LOAD)
+        return [
+            pltpu.make_async_copy(q_hbm.at[ex, :, cols], q.at[ex, :, cols], load_sem.at[0, ex, h]),
+            pltpu.make_async_copy(g_hbm.at[0, ex, :, cols], g.at[ex, :, cols], load_sem.at[1, ex, h]),
+            pltpu.make_async_copy(e_hbm.at[0, ex, :, cols], e.at[ex, :, cols], load_sem.at[2, ex, h]),
+        ]
+
     for ex in range(EXP):
-        for u in range(UNITS):
-            cols = pl.ds(u * UNIT, UNIT)
-            group = [
-                pltpu.make_async_copy(q_hbm.at[ex, :, cols], q.at[ex, :, cols], load_sem.at[0, ex, u]),
-                pltpu.make_async_copy(g_hbm.at[0, ex, :, cols], g.at[ex, :, cols], load_sem.at[1, ex, u]),
-                pltpu.make_async_copy(e_hbm.at[0, ex, :, cols], e.at[ex, :, cols], load_sem.at[2, ex, u]),
-            ]
-            for copy in group:
+        for h in range(LOADS):
+            for copy in loads(ex, h):
                 copy.start()
-            loads.append(group)
 
     barrier = pltpu.get_barrier_semaphore()
     greeted = [along(axis, d) for axis in (ax, ay, az) for d in (1, 2, 3)]
@@ -84,45 +87,50 @@
     for device in greeted:
         pl.semaphore_signal(barrier, inc=1, device_id=device, device_id_type=MESH)
 
-    sends = []
-    panel_recvs = []
-    for ex in range(EXP):
-        total = jnp.zeros((ROWS, 3 * R), jnp.float32)
-        for u in range(UNITS):
-            for copy in loads[ex * UNITS + u]:
+    def to_replica(ex, d):
+        spot = panels.at[ex, y]
+        return remote(spot, spot, ps.at[ex, d - 1], pr.at[ex, d - 1], along(ay, d))
+
+    def panel_term(ex, _):
+        def add(h, total):
+            for copy in loads(ex, h):
                 copy.wait()
-            cols = pl.ds(u * UNIT, UNIT)
+            cols = pl.ds(pl.multiple_of(h * LOAD, LOAD), LOAD)
             q3 = jnp.concatenate(split(q[ex, :, cols], 3), axis=0)
-            total += dot(g[ex, :, cols], q3, NT)
-            total += dot(e[ex, :, cols], q3, NT)
+            return total + (dot(g[ex, :, cols], q3, NT) + dot(e[ex, :, cols], q3, NT))
+
+        total = lax.fori_loop(0, LOADS, add, jnp.zeros((ROWS, 3 * R), jnp.float32))
         flat = jnp.concatenate([total, jnp.zeros((ROWS, R), jnp.float32)], axis=1).T
-        panels[ex, y] = flat[0:R] + flat[R : 2 * R] + flat[2 * R : 3 * R]
-        if ex == 0:
+        term = flat[0:R] + flat[R : 2 * R] + flat[2 * R : 3 * R]
+        panels[ex, y, 0:R] = term[:, 0:LANES]
+        panels[ex, y, R:] = jnp.concatenate([term[: R // 2, LANES:], term[R // 2 :, LANES:]], axis=1)
+
+        @pl.when(ex == 0)
+        def _():
             pl.semaphore_wait(barrier, len(greeted))
-        recvs = []
-        for d in (1, 2, 3):
-            copy = remote(panels.at[ex, y], panels.at[ex, y], ps.at[ex, d - 1], pr.at[ex, d - 1], along(ay, d))
-            copy.start()
-            sends.append(copy)
-            recvs.append(copy)
-        panel_recvs.append(recvs)
+
+        for d in (2, 1, 3):
+            to_replica(ex, d).start()
+        return 0
+
+    lax.fori_loop(0, EXP, panel_term, 0)
 
     def finish_panel(ex):
-        for copy in panel_recvs[ex]:
-            copy.wait_recv()
-        panel = (panels[ex, 0] + panels[ex, 1] + panels[ex, 2] + panels[ex, 3]) * (1.0 / REPS)
+        for d in (1, 2, 3):
+            to_replica(ex, d).wait_recv()
+        packed = (panels[ex, 0] + panels[ex, 1] + panels[ex, 2] + panels[ex, 3]) * (1.0 / REPS)
+        rest = packed[R:]
+        rest = jnp.concatenate([rest[:, : LANES // 2], rest[:, LANES // 2 :]], axis=0)
+        panel = jnp.concatenate([packed[0:R], rest], axis=1)
         left[ex] = jnp.concatenate(split(panel, 3), axis=0)
         return panel
 
     def product(ex, u):
-        def body(p, _):
-            cols = pl.ds(pl.multiple_of(u * UNIT + p * PIECE, PIECE), PIECE)
-            lhs = left[ex]
+        lhs = left[ex]
+        for p in range(SIDE):
+            cols = pl.ds(u * UNIT + p * PIECE, PIECE)
             both = dot(lhs, g[ex, :, cols]) + dot(lhs, e[ex, :, cols])
             part[ex, u, p] = both[0:R] + both[R : 2 * R] + both[2 * R : 3 * R]
-            return 0
-
-        lax.fori_loop(0, SIDE, body, 0)
 
     def to_partner(ex, u):
         return remote(part.at[ex, u], partner.at[u], cs.at[u], cr.at[u], other)
@@ -136,7 +144,7 @@
         to_partner(ex, u).wait_recv()
         for p in range(SIDE):
             part[ex, u, p] = part[ex, u, p] + partner[u, p]
-        for d in (1, 2, 3):
+        for d in (2, 1, 3):
             scatter1(ex, u, d).start()
 
     def coefficients(ex):
@@ -205,8 +213,18 @@
         mine = part[c, u, my(orders[u][0])] + r1[u, 0] + r1[u, 1] + r1[u, 2]
         for p in range(SIDE):
             s2[u, p] = mine[:, p * TILE : (p + 1) * TILE]
-        for d in (1, 2, 3):
+        for d in (2, 1, 3):
             scatter2(u, d).start()
+
+    def exchange3():
+        for u in range(UNITS):
+            for d in (1, 2, 3):
+                scatter2(u, d).wait_recv()
+            t3[u, my(orders[u][2])] = s2[u, my(orders[u][1])] + r2[u, 0] + r2[u, 1] + r2[u, 2]
+            for d in (2, 1, 3):
+                scatter3(u, d).start()
+
+    pl.when(c == 0)(exchange3)
 
     for copy in gram2_copies:
         copy.wait_recv()
@@ -231,12 +249,7 @@
     aug_ref[0] = inverses[0]
     aug_ref[1] = inverses[1]
 
-    for u in range(UNITS):
-        for d in (1, 2, 3):
-            scatter2(u, d).wait_recv()
-        t3[u, my(orders[u][2])] = s2[u, my(orders[u][1])] + r2[u, 0] + r2[u, 1] + r2[u, 2]
-        for d in (1, 2, 3):
-            scatter3(u, d).start()
+    pl.when(c == 1)(exchange3)
 
     for ex, panel in ((0, panel0), (1, panel1)):
         b = dot_high(inverses[ex], jnp.concatenate([panel] * 4, axis=0))
@@ -254,52 +267,74 @@
         spot = full.at[c, u, my(orders[u][0])]
         return remote(spot, spot, a1s.at[u, d - 1], a1r.at[u, d - 1], along(orders[u][0], d))
 
-    def forward(u):
-        return remote(full.at[c, u], full.at[c, u], fs.at[u], fr.at[u], other)
+    def forward(ex, u, d):
+        p = lax.rem(my(orders[u][0]) + d, SIDE)
+        return remote(full.at[ex, u, p], full.at[ex, u, p], fs.at[u, d], fr.at[u, d], other)
 
     for u in range(UNITS):
         for d in (1, 2, 3):
             scatter3(u, d).wait_recv()
         tile = t3[u, 0] + t3[u, 1] + t3[u, 2] + t3[u, 3]
         full[place(u)] = dot_high(aug_ref[c], jnp.concatenate([tile] * 4, axis=0)) * (1.0 / REPS)
-        for d in (1, 2, 3):
+        for d in (2, 1, 3):
             gather2(u, d).start()
     for u in range(UNITS):
         for d in (1, 2, 3):
             gather2(u, d).wait_recv()
-        for d in (1, 2, 3):
+        for d in (2, 1, 3):
             gather1(u, d).start()
+        forward(c, u, 0).start()
 
     def residual(ex, u):
-        def body(p, _):
-            cols = pl.ds(pl.multiple_of(u * UNIT + p * PIECE, PIECE), PIECE)
+        for p in range(SIDE):
+            cols = pl.ds(u * UNIT + p * PIECE, PIECE)
             new = jnp.concatenate([full[ex, u, p, i] for i in range(SIDE)], axis=1)
             coeffs[ex, :, cols] = new
             hi, lo = split(new, 2)
             low = dot(basis[ex], jnp.concatenate([hi, lo, hi, lo], axis=0))
             merged = g[ex, :, cols].astype(jnp.float32) + e[ex, :, cols].astype(jnp.float32)
             fresh[0, ex, :, cols] = (merged - low).astype(jnp.bfloat16)
-            return 0
-
-        lax.fori_loop(0, SIDE, body, 0)
-
-    for u in range(UNITS):
-        for d in (1, 2, 3):
+
+    def own_arrives(u):
+        for d in (1, 3, 2):
             gather1(u, d).wait_recv()
-        forward(u).start()
+            forward(c, u, SIDE - d).start()
+
+    def other_arrives(u):
+        for d in range(SIDE):
+            forward(1 - c, u, d).wait_recv()
+
+    for u in range(UNITS):
+        own_arrives(u)
         residual(c, u)
     for u in range(UNITS):
-        forward(u).wait_recv()
+        other_arrives(u)
         residual(1 - c, u)
 
-    for copy in sends + gram1_copies + gram2_copies:
+    for ex in range(EXP):
+        for d in (1, 2, 3):
+            to_replica(ex, d).wait_send()
+    for copy in gram1_copies + gram2_copies:
         copy.wait_send()
     for u in range(UNITS):
         to_partner(1 - c, u).wait_send()
-        forward(u).wait_send()
+        for d in range(SIDE):
+            forward(c, u, d).wait_send()
         for d in (1, 2, 3):
             for copy in (scatter1(c, u, d), scatter2(u, d), scatter3(u, d), gather2(u, d), gather1(u, d)):
                 copy.wait_send()
+
+
+def store(fresh, coeffs, fresh_out, coeffs_out, sem):
+    copies = [pltpu.make_async_copy(coeffs, coeffs_out, sem.at[EXP, 0])]
+    for ex in range(EXP):
+        for u in range(UNITS):
+            spot = (0, ex, slice(None), pl.ds(u * UNIT, UNIT))
+            copies.append(pltpu.make_async_copy(fresh.at[spot], fresh_out.at[spot], sem.at[ex, u]))
+    for copy in copies:
+        copy.start()
+    for copy in copies:
+        copy.wait()
 
 
 def shards(grads, errors, q_init):
@@ -307,11 +342,11 @@
     anywhere = pl.BlockSpec(memory_space=pl.ANY)
     vmem = pl.BlockSpec(memory_space=pltpu.VMEM)
     f32, b16 = jnp.float32, jnp.bfloat16
-    return pl.pallas_call(
+    fresh, coeffs = pl.pallas_call(
         kernel,
         out_shape=(
-            jax.ShapeDtypeStruct((1, EXP, ROWS, FF), b16),
-            jax.ShapeDtypeStruct((EXP, R, FF), f32),
+            pltpu.VMEM((1, EXP, ROWS, FF), b16),
+            pltpu.VMEM((EXP, R, FF), f32),
         ),
         in_specs=[anywhere] * 3,
         out_specs=(vmem, vmem),
@@ -319,7 +354,7 @@
             pltpu.VMEM((EXP, ROWS, FF), b16),
             pltpu.VMEM((EXP, ROWS, FF), b16),
             pltpu.VMEM((EXP, R, FF), f32),
-            pltpu.VMEM((EXP, REPS, R, ROWS), f32),
+            pltpu.VMEM((EXP, REPS, R + R // 2, LANES), f32),
             pltpu.VMEM((EXP, 3 * R, ROWS), b16),
             pltpu.VMEM((EXP, ROWS, 4 * R), b16),
             pltpu.VMEM((2 * SIDE, R, 4 * R), f32),
@@ -332,7 +367,7 @@
             pltpu.VMEM((UNITS, SIDE - 1, R, TILE), f32),
             pltpu.VMEM((UNITS, SIDE, R, TILE), f32),
             pltpu.VMEM((EXP, UNITS, SIDE, SIDE, R, TILE), f32),
-            dma((3, EXP, UNITS)),
+            dma((3, EXP, LOADS)),
             dma((EXP, 3)), dma((EXP, 3)),
             dma((7,)), dma((7,)), dma((3,)), dma((3,)),
             dma((UNITS,)), dma((UNITS,)),
@@ -341,14 +376,26 @@
             dma((UNITS, 3)), dma((UNITS, 3)),
             dma((UNITS, 3)), dma((UNITS, 3)),
             dma((UNITS, 3)), dma((UNITS, 3)),
-            dma((UNITS,)), dma((UNITS,)),
+            dma((UNITS, SIDE)), dma((UNITS, SIDE)),
         ],
         compiler_params=pltpu.CompilerParams(
-            collective_id=0, has_side_effects=True, vmem_limit_bytes=56 * 2**20
+            collective_id=0, has_side_effects=True, vmem_limit_bytes=48 * 2**20
         ),
         cost_estimate=pl.CostEstimate(flops=10**9, bytes_accessed=25 * 10**6, transcendentals=0),
         name="compress",
     )(grads, errors, q_init)
+    return pl.pallas_call(
+        store,
+        out_shape=(
+            jax.ShapeDtypeStruct((1, EXP, ROWS, FF), b16),
+            jax.ShapeDtypeStruct((EXP, R, FF), f32),
+        ),
+        in_specs=[anywhere] * 2,
+        out_specs=(anywhere, anywhere),
+        scratch_shapes=[dma((EXP + 1, UNITS))],
+        compiler_params=pltpu.CompilerParams(has_side_effects=True, vmem_limit_bytes=2**20),
+        name="store",
+    )(fresh, coeffs)
 
 
 def solution(mesh):

time: 62.6 us -> 49.8 us (0.80)
  local copies, waits for them, and re-layouts: 7.67 us -> 0 us
  Pallas kernels: 54.2 us -> 49 us
    unnamed x4 -> x0, local copies, waits for them, and re-layouts: 7.67 us -> none
    pallas_call x1 -> x2, Pallas kernels: 54.2 us -> 49 us  [the longest x1 45.6 us: shards(): pl.pallas_call(kernel, out_shape=(pltpu.VMEM((1, EXP, ROWS, FF), b16), pl...]
where the time goes in v2:
time: 49.8 us; the launch traced here: 49.6 us
  Pallas kernels  49 us (98%)
  between operations  0.64 us (1%)
    pallas_call x1, Pallas kernels, shards(): pl.pallas_call(kernel, out_shape=(pltpu.VMEM((1, EXP, ROWS, FF), b16), pl...  45.6 us
    pallas_call x1, Pallas kernels, shards(): pl.pallas_call(store, out_shape=(jax.ShapeDtypeStruct((1, EXP, ROWS, FF),...  3.4 us

profile of v2, /device:TPU:1, one launch (start us, length us, event | category | flops | bytes accessed | tf_op | source)
XLA Modules:
  0.0 49.6 jit_solution(8740142497884596143)
XLA Ops:
  0.6 45.6 %compress.1 = (bf16[1,2,192,8192]{3,2,1,0:T(8,128)(2,1)S(1)}, f32[2,32,8192]{2,1,0:T(8,128)S(1)}) custom-call(bf16[1,2,192,8192]{3,2,1,0:T(8,128)(2,1)} %g_hbm.1, bf16[1,2,192,8192]{3,2,1,0:T(8,128)(2,1)} %e_hbm.1, f32[2,32,8192]{2,1,0:T(8,128)} %q_hbm.1), custom_call_target="tpu_custom_call" | custom-call | flops 1000000000 | bytes 25000000 | tf_op jit(solution)/shard_map/compress/pallas_call | solution.py:345
  46.2 3.4 %store.1 = (bf16[1,2,192,8192]{3,2,1,0:T(8,128)(2,1)}, f32[2,32,8192]{2,1,0:T(8,128)}) custom-call(bf16[1,2,192,8192]{3,2,1,0:T(8,128)(2,1)S(1)} %get-tuple-element.4.fresh, f32[2,32,8192]{2,1,0:T(8,128)S(1)} %get-tuple-element.5.coeffs), custom_call_target="tpu_custom_call" | custom-call | tf_op jit(solution)/shard_map/store/pallas_call | solution.py:387

commit v3 on v2

v3 whole, which is shorter than its diff:
```python
import jax
import jax.numpy as jnp
from jax import lax
from jax.experimental import pallas as pl
from jax.experimental.pallas import tpu as pltpu
from jax.sharding import PartitionSpec as P

EXP, ROWS, FF, R = 2, 192, 8192, 32
REPS, SIDE = 4, 4
UNITS = 4
UNIT = FF // UNITS
PIECE = UNIT // SIDE
TILE = PIECE // SIDE
LANES = 128
LOADS = 2
LOAD = FF // LOADS
MESH = pl.DeviceIdType.MESH
HIGH = lax.Precision.HIGHEST
NN = (((1,), (0,)), ((), ()))
NT = (((1,), (1,)), ((), ()))


def split(value, pieces):
    out = []
    for _ in range(pieces):
        piece = value.astype(jnp.bfloat16)
        out.append(piece)
        value = value - piece.astype(jnp.float32)
    return out


def dot(a, b, dims=NN):
    return lax.dot_general(a, b, dims, preferred_element_type=jnp.float32)


def dot_high(a, b, dims=NN):
    return lax.dot_general(a, b, dims, precision=HIGH, preferred_element_type=jnp.float32)


def kernel(
    g_hbm, e_hbm, q_hbm, fresh, coeffs, g, e, basis,
    q, panels, left, gram1, gram2, aug_ref, part, partner, r1, s2, r2, t3, full,
    load_sem, ps, pr, g1s, g1r, g2s, g2r, cs, cr, s1s, s1r, s2s, s2r, s3s, s3r, a2s, a2r, a1s, a1r, fs, fr,
):
    y = lax.axis_index("rep")
    row = lax.axis_index("row")
    c = lax.rem(row, 2)
    z = lax.rem(row // 2, SIDE)
    x = row // (2 * SIDE)
    me = (x, y, z)

    def at(place, core):
        return (place[1], place[0] * (2 * SIDE) + place[2] * 2 + core)

    def along(axis, d):
        return at([lax.rem(p + d * w, SIDE) for p, w in zip(me, axis)], c)

    def my(axis):
        return x * axis[0] + y * axis[1] + z * axis[2]

    ax, ay, az = (1, 0, 0), (0, 1, 0), (0, 0, 1)

    def either(first, second):
        return [tuple(a * (1 - c) + b * c for a, b in zip(p, q)) for p, q in zip(first, second)]

    orders = [
        either((ax, ay, az), (az, ax, ay)),
        either((ay, az, ax), (ax, az, ay)),
        either((ay, az, ax), (ax, ay, az)),
        either((az, ax, ay), (ay, ax, az)),
    ]
    other = at(me, 1 - c)

    def remote(src, dst, send, recv, device):
        return pltpu.make_async_remote_copy(
            src_ref=src, dst_ref=dst, send_sem=send, recv_sem=recv, device_id=device, device_id_type=MESH
        )

    barrier = pltpu.get_barrier_semaphore()
    greeted = [along(axis, d) for axis in (ax, ay, az) for d in (1, 2, 3)]
    greeted += [at((lax.rem(x + d, SIDE), y, z), 1 - c) for d in range(SIDE)]
    for device in greeted:
        pl.semaphore_signal(barrier, inc=1, device_id=device, device_id_type=MESH)

    def loads(ex, h):
        cols = pl.ds(pl.multiple_of(h * LOAD, LOAD), LOAD)
        return [
            pltpu.make_async_copy(q_hbm.at[ex, :, cols], q.at[ex, :, cols], load_sem.at[0, ex, h]),
            pltpu.make_async_copy(g_hbm.at[0, ex, :, cols], g.at[ex, :, cols], load_sem.at[1, ex, h]),
            pltpu.make_async_copy(e_hbm.at[0, ex, :, cols], e.at[ex, :, cols], load_sem.at[2, ex, h]),
        ]

    for ex in range(EXP):
        for h in range(LOADS):
            for copy in loads(ex, h):
                copy.start()

    def to_replica(ex, d):
        spot = panels.at[ex, y]
        return remote(spot, spot, ps.at[ex, d - 1], pr.at[ex, d - 1], along(ay, d))

    def panel_term(ex, _):
        def add(h, total):
            for copy in loads(ex, h):
                copy.wait()
            cols = pl.ds(pl.multiple_of(h * LOAD, LOAD), LOAD)
            q3 = jnp.concatenate(split(q[ex, :, cols], 3), axis=0)
            return total + (dot(g[ex, :, cols], q3, NT) + dot(e[ex, :, cols], q3, NT))

        total = lax.fori_loop(0, LOADS, add, jnp.zeros((ROWS, 3 * R), jnp.float32))
        flat = jnp.concatenate([total, jnp.zeros((ROWS, R), jnp.float32)], axis=1).T
        term = flat[0:R] + flat[R : 2 * R] + flat[2 * R : 3 * R]
        panels[ex, y, 0:R] = term[:, 0:LANES]
        panels[ex, y, R:] = jnp.concatenate([term[: R // 2, LANES:], term[R // 2 :, LANES:]], axis=1)

        @pl.when(ex == 0)
        def _():
            pl.semaphore_wait(barrier, len(greeted))

        for d in (2, 1, 3):
            to_replica(ex, d).start()
        return 0

    lax.fori_loop(0, EXP, panel_term, 0)

    def finish_panel(ex):
        for d in (1, 2, 3):
            to_replica(ex, d).wait_recv()
        packed = (panels[ex, 0] + panels[ex, 1] + panels[ex, 2] + panels[ex, 3]) * (1.0 / REPS)
        rest = packed[R:]
        rest = jnp.concatenate([rest[:, : LANES // 2], rest[:, LANES // 2 :]], axis=0)
        panel = jnp.concatenate([packed[0:R], rest], axis=1)
        left[ex] = jnp.concatenate(split(panel, 3), axis=0)
        return panel

    def unit(j):
        return j // 2, 2 * c + j % 2

    def unit_there(j):
        return j // 2, 2 * (1 - c) + j % 2

    def product(ex, u, p):
        cols = pl.ds(pl.multiple_of(u * UNIT + p * PIECE, PIECE), PIECE)
        both = dot(left[ex], g[ex, :, cols]) + dot(left[ex], e[ex, :, cols])
        part[ex, u, p] = both[0:R] + both[R : 2 * R] + both[2 * R : 3 * R]

    def to_partner(j, p):
        spot = part.at[(*unit_there(j), p)]
        return remote(spot, partner.at[j, p], cs.at[j, p], cr.at[j, p], other)

    def scatter1(j, d):
        axis = orders[j][0]
        p = lax.rem(my(axis) + d, SIDE)
        spot = part.at[(*unit(j), p)]
        return remote(spot, r1.at[j, d - 1], s1s.at[j, d - 1], s1r.at[j, d - 1], along(axis, d))

    def coefficients(ex):
        for j in (2 * ex, 2 * ex + 1):
            for p in range(SIDE):
                product(*unit_there(j), p)
            for p in range(SIDE):
                to_partner(j, p).start()
        for j in (2 * ex, 2 * ex + 1):
            for p in range(SIDE):
                product(*unit(j), p)
            for p in range(SIDE):
                to_partner(j, p).wait_recv()
                spot = (*unit(j), p)
                part[spot] = part[spot] + partner[j, p]
            for d in (2, 1, 3):
                scatter1(j, d).start()

    panel0 = finish_panel(0)
    coefficients(0)
    panel1 = finish_panel(1)

    zeros = jnp.zeros((R, ROWS), jnp.float32)
    pad0 = jnp.concatenate([panel0, zeros, zeros, zeros], axis=0)
    pad1 = jnp.concatenate([zeros, zeros, panel1, zeros], axis=0)
    gram1[2 * x + c] = dot_high(panel0, pad0, NT) + dot_high(panel1, pad1, NT)
    gram1_copies = []
    for i in range(7):
        if i < 3:
            device = along(ax, i + 1)
        else:
            device = at((lax.rem(x + i - 3, SIDE), y, z), 1 - c)
        copy = remote(gram1.at[2 * x + c], gram1.at[2 * x + c], g1s.at[i], g1r.at[i], device)
        copy.start()
        gram1_copies.append(copy)

    coefficients(1)

    def scatter2(j, d):
        axis = orders[j][1]
        p = lax.rem(my(axis) + d, SIDE)
        return remote(s2.at[j, p], r2.at[j, d - 1], s2s.at[j, d - 1], s2r.at[j, d - 1], along(axis, d))

    def scatter3(j, d):
        axis = orders[j][2]
        i = my(axis)
        return remote(t3.at[j, i], t3.at[j, i], s3s.at[j, d - 1], s3r.at[j, d - 1], along(axis, d))

    def gather2(j, d):
        spot = full.at[(*unit(j), my(orders[j][0]), my(orders[j][1]))]
        return remote(spot, spot, a2s.at[j, d - 1], a2r.at[j, d - 1], along(orders[j][1], d))

    def gather1(j, d):
        spot = full.at[(*unit(j), my(orders[j][0]))]
        return remote(spot, spot, a1s.at[j, d - 1], a1r.at[j, d - 1], along(orders[j][0], d))

    def forward(j, d):
        spot = full.at[(*unit(j), lax.rem(my(orders[j][0]) + d, SIDE))]
        return remote(spot, spot, fs.at[j, d], fr.at[j, d], other)

    def exchange2(ex):
        for j in (2 * ex, 2 * ex + 1):
            for d in (1, 3, 2):
                scatter1(j, d).wait_recv()
            mine = part[(*unit(j), my(orders[j][0]))] + r1[j, 0] + r1[j, 1] + r1[j, 2]
            for p in range(SIDE):
                s2[j, p] = mine[:, p * TILE : (p + 1) * TILE]
            for d in (2, 1, 3):
                scatter2(j, d).start()

    def exchange3(ex):
        for j in (2 * ex, 2 * ex + 1):
            for d in (1, 3, 2):
                scatter2(j, d).wait_recv()
            t3[j, my(orders[j][2])] = s2[j, my(orders[j][1])] + r2[j, 0] + r2[j, 1] + r2[j, 2]
            for d in (2, 1, 3):
                scatter3(j, d).start()

    def own_tile(ex):
        for j in (2 * ex, 2 * ex + 1):
            for d in (1, 3, 2):
                scatter3(j, d).wait_recv()
            tile = t3[j, 0] + t3[j, 1] + t3[j, 2] + t3[j, 3]
            new = dot_high(aug_ref[ex], jnp.concatenate([tile] * 4, axis=0)) * (1.0 / REPS)
            full[(*unit(j), my(orders[j][0]), my(orders[j][1]))] = new
            for d in (2, 1, 3):
                gather2(j, d).start()

    def spread(ex):
        for j in (2 * ex, 2 * ex + 1):
            for d in (1, 3, 2):
                gather2(j, d).wait_recv()
            for d in (2, 1, 3):
                gather1(j, d).start()
            forward(j, 0).start()

    for copy in gram1_copies:
        copy.wait_recv()
    total = gram1[0]
    for i in range(1, 2 * SIDE):
        total += gram1[i]
    gram2[z] = total
    gram2_copies = []
    for d in (2, 1, 3):
        copy = remote(gram2.at[z], gram2.at[z], g2s.at[d - 1], g2r.at[d - 1], along(az, d))
        copy.start()
        gram2_copies.append(copy)

    exchange2(0)
    exchange2(1)
    exchange3(0)

    for copy in gram2_copies:
        copy.wait_recv()
    aug = gram2[0] + gram2[1] + gram2[2] + gram2[3]
    rows_at = lax.broadcasted_iota(jnp.int32, (R, 4 * R), 0)
    lanes_at = lax.broadcasted_iota(jnp.int32, (R, 4 * R), 1)
    unit_at = (lanes_at == rows_at + R) | (lanes_at == rows_at + 3 * R)
    aug = jnp.where(unit_at, 1.0, aug)
    first = lanes_at < 2 * R
    pivots = jnp.ones((R, 4 * R), jnp.float32)
    for k in range(0, R, 2):
        col = [jnp.where(first, aug[:, i : i + 1], aug[:, 2 * R + i : 2 * R + i + 1]) for i in (k, k + 1)]
        row = [aug[i : i + 1, :] for i in (k, k + 1)]
        top, side, low = col[0][k : k + 1, :], col[0][k + 1 : k + 2, :], col[1][k + 1 : k + 2, :]
        scale = side / top
        ratio = row[0] / top
        below = row[1] - scale * row[0]
        pivot = low - scale * side
        col[1] = col[1] - col[0] * scale
        pivots = jnp.where(rows_at == k, top, jnp.where(rows_at == k + 1, pivot, pivots))
        rest = aug - col[0] * ratio - col[1] * (below / pivot)
        aug = jnp.where(rows_at > k + 1, rest, jnp.where(rows_at == k + 1, below, aug))
    aug = aug / jnp.sqrt(pivots)
    for ex in range(EXP):
        wanted = (lanes_at >= (2 * ex + 1) * R) & (lanes_at < (2 * ex + 2) * R)
        aug_ref[ex] = jnp.where(wanted, aug, 0.0)

    exchange3(1)
    own_tile(0)

    for ex, panel in ((0, panel0), (1, panel1)):
        b = dot_high(aug_ref[ex], jnp.concatenate([panel] * 4, axis=0))
        hi, lo = [piece.astype(jnp.float32) for piece in split(b, 2)]
        basis[ex] = jnp.concatenate([hi, hi, lo, lo], axis=0).T.astype(jnp.bfloat16)

    own_tile(1)
    spread(0)
    spread(1)

    def finish_unit(ex, u):
        for p in range(SIDE):
            cols = pl.ds(pl.multiple_of(u * UNIT + p * PIECE, PIECE), PIECE)
            coeffs[ex, :, cols] = jnp.concatenate([full[ex, u, p, i] for i in range(SIDE)], axis=1)
            if ex == 0:
                fresh[:, cols] = residual(g, e, basis, coeffs, ex, cols)

    for ex in range(EXP):
        for j in (2 * ex, 2 * ex + 1):
            for d in (1, 3, 2):
                gather1(j, d).wait_recv()
                forward(j, SIDE - d).start()
            finish_unit(*unit(j))
        for j in (2 * ex, 2 * ex + 1):
            for d in range(SIDE):
                forward(j, d).wait_recv()
            finish_unit(*unit_there(j))

    for ex in range(EXP):
        for d in (1, 2, 3):
            to_replica(ex, d).wait_send()
    for copy in gram1_copies + gram2_copies:
        copy.wait_send()
    for j in range(UNITS):
        for d in range(SIDE):
            to_partner(j, d).wait_send()
            forward(j, d).wait_send()
        for d in (1, 2, 3):
            for copy in (scatter1(j, d), scatter2(j, d), scatter3(j, d), gather2(j, d), gather1(j, d)):
                copy.wait_send()


def residual(g, e, basis, coeffs, ex, cols):
    hi, lo = split(coeffs[ex, :, cols], 2)
    low = dot(basis[ex], jnp.concatenate([hi, lo, hi, lo], axis=0))
    merged = g[ex, :, cols].astype(jnp.float32) + e[ex, :, cols].astype(jnp.float32)
    return (merged - low).astype(jnp.bfloat16)


def store(fresh0, coeffs, g, e, basis, fresh_out, coeffs_out, fresh1, sem):
    copies = []

    def send(src, dst):
        copies.append(pltpu.make_async_copy(src, dst, sem.at[len(copies)]))
        copies[-1].start()

    units = [pl.ds(u * UNIT, UNIT) for u in range(UNITS)]
    for cols in units:
        send(fresh0.at[:, cols], fresh_out.at[0, 0, :, cols])
    for ex in range(EXP):
        send(coeffs.at[ex], coeffs_out.at[ex])
    for u in range(UNITS):
        for p in range(SIDE):
            cols = pl.ds(u * UNIT + p * PIECE, PIECE)
            fresh1[:, cols] = residual(g, e, basis, coeffs, 1, cols)
        send(fresh1.at[:, units[u]], fresh_out.at[0, 1, :, units[u]])
    for copy in copies:
        copy.wait()


def shards(grads, errors, q_init):
    dma = pltpu.SemaphoreType.DMA
    anywhere = pl.BlockSpec(memory_space=pl.ANY)
    vmem = pl.BlockSpec(memory_space=pltpu.VMEM)
    f32, b16 = jnp.float32, jnp.bfloat16
    held = pl.pallas_call(
        kernel,
        out_shape=(
            pltpu.VMEM((ROWS, FF), b16),
            pltpu.VMEM((EXP, R, FF), f32),
            pltpu.VMEM((EXP, ROWS, FF), b16),
            pltpu.VMEM((EXP, ROWS, FF), b16),
            pltpu.VMEM((EXP, ROWS, 4 * R), b16),
        ),
        in_specs=[anywhere] * 3,
        out_specs=(vmem,) * 5,
        scratch_shapes=[
            pltpu.VMEM((EXP, R, FF), f32),
            pltpu.VMEM((EXP, REPS, R + R // 2, LANES), f32),
            pltpu.VMEM((EXP, 3 * R, ROWS), b16),
            pltpu.VMEM((2 * SIDE, R, 4 * R), f32),
            pltpu.VMEM((SIDE, R, 4 * R), f32),
            pltpu.VMEM((EXP, R, 4 * R), f32),
            pltpu.VMEM((EXP, UNITS, SIDE, R, PIECE), f32),
            pltpu.VMEM((UNITS, SIDE, R, PIECE), f32),
            pltpu.VMEM((UNITS, SIDE - 1, R, PIECE), f32),
            pltpu.VMEM((UNITS, SIDE, R, TILE), f32),
            pltpu.VMEM((UNITS, SIDE - 1, R, TILE), f32),
            pltpu.VMEM((UNITS, SIDE, R, TILE), f32),
            pltpu.VMEM((EXP, UNITS, SIDE, SIDE, R, TILE), f32),
            dma((3, EXP, LOADS)),
            dma((EXP, 3)), dma((EXP, 3)),
            dma((7,)), dma((7,)), dma((3,)), dma((3,)),
            dma((UNITS, SIDE)), dma((UNITS, SIDE)),
            dma((UNITS, 3)), dma((UNITS, 3)),
            dma((UNITS, 3)), dma((UNITS, 3)),
            dma((UNITS, 3)), dma((UNITS, 3)),
            dma((UNITS, 3)), dma((UNITS, 3)),
            dma((UNITS, 3)), dma((UNITS, 3)),
            dma((UNITS, SIDE)), dma((UNITS, SIDE)),
        ],
        compiler_params=pltpu.CompilerParams(
            collective_id=0, has_side_effects=True, vmem_limit_bytes=44 * 2**20
        ),
        cost_estimate=pl.CostEstimate(flops=10**9, bytes_accessed=25 * 10**6, transcendentals=0),
        name="compress",
    )(grads, errors, q_init)
    return pl.pallas_call(
        store,
        out_shape=(
            jax.ShapeDtypeStruct((1, EXP, ROWS, FF), b16),
            jax.ShapeDtypeStruct((EXP, R, FF), f32),
        ),
        in_specs=[anywhere] + [vmem] * 4,
        out_specs=(anywhere, anywhere),
        scratch_shapes=[pltpu.VMEM((ROWS, FF), b16), dma((2 * UNITS + EXP,))],
        compiler_params=pltpu.CompilerParams(has_side_effects=True, vmem_limit_bytes=8 * 2**20),
        name="store",
    )(*held)


def solution(mesh):
    in_specs = (P("rep", None, "row", None), P("rep", None, "row", None), P())
    out_specs = (P("rep", None, "row", None), P())
    return jax.shard_map(shards, mesh=mesh, in_specs=in_specs, out_specs=out_specs, check_vma=False)
```

time: 49.8 us -> 48.6 us (0.976)
  Pallas kernels: 49 us -> 47.9 us
    pallas_call x1, Pallas kernels: 45.6 us -> 44.5 us  [shards(): pl.pallas_call(kernel, out_shape=(pltpu.VMEM((ROWS, FF), b16), pltpu.VMEM...]
where the time goes in v3:
time: 48.6 us; the launch traced here: 48.5 us
  Pallas kernels  47.9 us (99%)
  between operations  0.64 us (1%)
    pallas_call x1, Pallas kernels, shards(): pl.pallas_call(kernel, out_shape=(pltpu.VMEM((ROWS, FF), b16), pltpu.VMEM...  44.5 us
    pallas_call x1, Pallas kernels, shards(): pl.pallas_call(store, out_shape=(jax.ShapeDtypeStruct((1, EXP, ROWS, FF),...  3.38 us

profile of v3, /device:TPU:1, one launch (start us, length us, event | category | flops | bytes accessed | tf_op | source)
XLA Modules:
  0.0 48.5 jit_solution(10289551167970347973)
XLA Ops:
  0.6 44.5 %compress.1 = (bf16[192,8192]{1,0:T(8,128)(2,1)S(1)}, f32[2,32,8192]{2,1,0:T(8,128)S(1)}, bf16[2,192,8192]{2,1,0:T(8,128)(2,1)S(1)}, bf16[2,192,8192]{2,1,0:T(8,128)(2,1)S(1)}, bf16[2,192,128]{2,1,0:T(8,128)(2,1)S(1)}) custom-call(bf16[1,2,192,8192]{3,2,1,0:T(8,128)(2,1)} %g_hbm.1, bf16[1,2,192,8192]{3,2,1,0:T(8,128)(2,1)} %e_hbm.1, f32[2,32,8192]{2,1,0:T(8,128)} %q_hbm.1), custom_call_target="tpu_custom_call" | custom-call | flops 1000000000 | bytes 25000000 | tf_op jit(solution)/shard_map/compress/pallas_call | solution.py:370
  45.2 3.4 %store.1 = (bf16[1,2,192,8192]{3,2,1,0:T(8,128)(2,1)}, f32[2,32,8192]{2,1,0:T(8,128)}) custom-call(bf16[192,8192]{1,0:T(8,128)(2,1)S(1)} %get-tuple-element.7.fresh0, f32[2,32,8192]{2,1,0:T(8,128)S(1)} %get-tuple-element.8.coeffs, bf16[2,192,8192]{2,1,0:T(8,128)(2,1)S(1)} %get-tuple-element.9.g, bf16[2,192,8192]{2,1,0:T(8,128)(2,1)S(1)} %get-tuple-element.10.e, ...), custom_call_target="tpu_custom_call" | custom-call | tf_op jit(solution)/shard_map/store/pallas_call | solution.py:412

commit v4 on v3

--- a/solution.py
+++ b/solution.py
@@ -8,11 +8,12 @@
 EXP, ROWS, FF, R = 2, 192, 8192, 32
 REPS, SIDE = 4, 4
 UNITS = 4
+STREAMS = 6
 UNIT = FF // UNITS
 PIECE = UNIT // SIDE
 TILE = PIECE // SIDE
 LANES = 128
-LOADS = 2
+LOADS = 4
 LOAD = FF // LOADS
 MESH = pl.DeviceIdType.MESH
 HIGH = lax.Precision.HIGHEST
@@ -39,7 +40,7 @@
 
 def kernel(
     g_hbm, e_hbm, q_hbm, fresh, coeffs, g, e, basis,
-    q, panels, left, gram1, gram2, aug_ref, part, partner, r1, s2, r2, t3, full,
+    q, panels, left, gram1, gram2, aug_ref, part, partner, r1, r1b, s2, r2, t3, full,
     load_sem, ps, pr, g1s, g1r, g2s, g2r, cs, cr, s1s, s1r, s2s, s2r, s3s, s3r, a2s, a2r, a1s, a1r, fs, fr,
 ):
     y = lax.axis_index("rep")
@@ -60,15 +61,35 @@
 
     ax, ay, az = (1, 0, 0), (0, 1, 0), (0, 0, 1)
 
-    def either(first, second):
-        return [tuple(a * (1 - c) + b * c for a, b in zip(p, q)) for p, q in zip(first, second)]
-
-    orders = [
-        either((ax, ay, az), (az, ax, ay)),
-        either((ay, az, ax), (ax, az, ay)),
-        either((ay, az, ax), (ax, ay, az)),
-        either((az, ax, ay), (ay, ax, az)),
+    def either(first, second, core=c):
+        return [tuple(a * (1 - core) + b * core for a, b in zip(p, q)) for p, q in zip(first, second)]
+
+    table = [
+        ((ax, ay, az), (ay, az, ax)),
+        ((az, ax, ay), (az, ay, ax)),
+        ((ay, az, ax), (az, ax, ay)),
+        ((ax, ay, az), (ax, az, ay)),
     ]
+    orders = [either(*pair) for pair in table]
+    orders_there = [either(*pair, 1 - c) for pair in table]
+    streams = []
+    for j in range(UNITS):
+        if j % 2 == 0:
+            streams.append((j, pl.ds(0, R), 0, 1))
+        else:
+            streams.append((j, pl.ds(0, R // 2), 0, 1))
+            streams.append((j, pl.ds(R // 2, R // 2), 1, 0))
+
+    def streams_of(ex):
+        return [s for s, stream in enumerate(streams) if stream[0] // 2 == ex]
+
+    def axes(s):
+        j, _, a, b = streams[s]
+        return orders[j][a], orders[j][b]
+
+    def shifted(axis, d):
+        return lax.rem(my(axis) + d, SIDE)
+
     other = at(me, 1 - c)
 
     def remote(src, dst, send, recv, device):
@@ -148,27 +169,41 @@
         spot = part.at[(*unit_there(j), p)]
         return remote(spot, partner.at[j, p], cs.at[j, p], cr.at[j, p], other)
 
-    def scatter1(j, d):
-        axis = orders[j][0]
-        p = lax.rem(my(axis) + d, SIDE)
-        spot = part.at[(*unit(j), p)]
-        return remote(spot, r1.at[j, d - 1], s1s.at[j, d - 1], s1r.at[j, d - 1], along(axis, d))
+    def lanes(p):
+        return pl.ds(pl.multiple_of(p * TILE, TILE), TILE)
+
+    def scatter1(s, d):
+        j, rows, swapped, _ = streams[s]
+        axis = axes(s)[0]
+        p = shifted(axis, d)
+        if swapped:
+            src, dst = part.at[(*unit(j), slice(None), rows, lanes(p))], r1b.at[j // 2, d - 1]
+        else:
+            src, dst = part.at[(*unit(j), p, rows)], r1.at[j, d - 1, rows]
+        return remote(src, dst, s1s.at[s, d - 1], s1r.at[s, d - 1], along(axis, d))
 
     def coefficients(ex):
-        for j in (2 * ex, 2 * ex + 1):
+        units = (2 * ex, 2 * ex + 1)
+        for j in units:
             for p in range(SIDE):
                 product(*unit_there(j), p)
-            for p in range(SIDE):
-                to_partner(j, p).start()
-        for j in (2 * ex, 2 * ex + 1):
+            for d in (2, 1, 3, 0):
+                to_partner(j, shifted(orders_there[j][0], d)).start()
+        for j in units:
             for p in range(SIDE):
                 product(*unit(j), p)
-            for p in range(SIDE):
+        for j in units:
+            mine = [s for s in streams_of(ex) if streams[s][0] == j]
+            for d in (2, 1, 3, 0):
+                p = shifted(orders[j][0], d)
                 to_partner(j, p).wait_recv()
                 spot = (*unit(j), p)
                 part[spot] = part[spot] + partner[j, p]
-            for d in (2, 1, 3):
-                scatter1(j, d).start()
+                if d:
+                    scatter1(mine[0], d).start()
+            for s in mine[1:]:
+                for d in (2, 1, 3):
+                    scatter1(s, d).start()
 
     panel0 = finish_panel(0)
     coefficients(0)
@@ -190,43 +225,64 @@
 
     coefficients(1)
 
-    def scatter2(j, d):
-        axis = orders[j][1]
-        p = lax.rem(my(axis) + d, SIDE)
-        return remote(s2.at[j, p], r2.at[j, d - 1], s2s.at[j, d - 1], s2r.at[j, d - 1], along(axis, d))
+    def scatter2(s, d):
+        j, rows, _, _ = streams[s]
+        axis = axes(s)[1]
+        src, dst = s2.at[j, shifted(axis, d), rows], r2.at[j, d - 1, rows]
+        return remote(src, dst, s2s.at[s, d - 1], s2r.at[s, d - 1], along(axis, d))
 
     def scatter3(j, d):
         axis = orders[j][2]
         i = my(axis)
         return remote(t3.at[j, i], t3.at[j, i], s3s.at[j, d - 1], s3r.at[j, d - 1], along(axis, d))
 
-    def gather2(j, d):
-        spot = full.at[(*unit(j), my(orders[j][0]), my(orders[j][1]))]
-        return remote(spot, spot, a2s.at[j, d - 1], a2r.at[j, d - 1], along(orders[j][1], d))
-
-    def gather1(j, d):
-        spot = full.at[(*unit(j), my(orders[j][0]))]
-        return remote(spot, spot, a1s.at[j, d - 1], a1r.at[j, d - 1], along(orders[j][0], d))
-
-    def forward(j, d):
-        spot = full.at[(*unit(j), lax.rem(my(orders[j][0]) + d, SIDE))]
-        return remote(spot, spot, fs.at[j, d], fr.at[j, d], other)
+    def gather2(s, d):
+        j, rows, _, _ = streams[s]
+        axis = axes(s)[1]
+        spot = full.at[(*unit(j), my(orders[j][0]), my(orders[j][1]), rows)]
+        return remote(spot, spot, a2s.at[s, d - 1], a2r.at[s, d - 1], along(axis, d))
+
+    def band(s, p):
+        j, rows, swapped, _ = streams[s]
+        if swapped:
+            return full.at[(*unit(j), slice(None), p, rows)]
+        return full.at[(*unit(j), p, slice(None), rows)]
+
+    def gather1(s, d):
+        axis = axes(s)[0]
+        spot = band(s, my(axis))
+        return remote(spot, spot, a1s.at[s, d - 1], a1r.at[s, d - 1], along(axis, d))
+
+    def forward(s, d):
+        spot = band(s, shifted(axes(s)[0], d))
+        return remote(spot, spot, fs.at[s, d], fr.at[s, d], other)
 
     def exchange2(ex):
-        for j in (2 * ex, 2 * ex + 1):
+        for s in streams_of(ex):
+            j, rows, swapped, _ = streams[s]
             for d in (1, 3, 2):
-                scatter1(j, d).wait_recv()
-            mine = part[(*unit(j), my(orders[j][0]))] + r1[j, 0] + r1[j, 1] + r1[j, 2]
-            for p in range(SIDE):
-                s2[j, p] = mine[:, p * TILE : (p + 1) * TILE]
+                scatter1(s, d).wait_recv()
+            p = my(axes(s)[0])
+            if swapped:
+                for i in range(SIDE):
+                    mine = part[(*unit(j), i, rows, lanes(p))]
+                    s2[j, i, rows] = mine + r1b[ex, 0, i] + r1b[ex, 1, i] + r1b[ex, 2, i]
+            else:
+                mine = part[(*unit(j), p, rows)] + r1[j, 0, rows] + r1[j, 1, rows] + r1[j, 2, rows]
+                for i in range(SIDE):
+                    s2[j, i, rows] = mine[:, i * TILE : (i + 1) * TILE]
             for d in (2, 1, 3):
-                scatter2(j, d).start()
+                scatter2(s, d).start()
 
     def exchange3(ex):
         for j in (2 * ex, 2 * ex + 1):
-            for d in (1, 3, 2):
-                scatter2(j, d).wait_recv()
-            t3[j, my(orders[j][2])] = s2[j, my(orders[j][1])] + r2[j, 0] + r2[j, 1] + r2[j, 2]
+            for s in streams_of(ex):
+                if streams[s][0] == j:
+                    rows = streams[s][1]
+                    for d in (1, 3, 2):
+                        scatter2(s, d).wait_recv()
+                    mine = s2[j, my(axes(s)[1]), rows]
+                    t3[j, my(orders[j][2]), rows] = mine + r2[j, 0, rows] + r2[j, 1, rows] + r2[j, 2, rows]
             for d in (2, 1, 3):
                 scatter3(j, d).start()
 
@@ -237,17 +293,20 @@
             tile = t3[j, 0] + t3[j, 1] + t3[j, 2] + t3[j, 3]
             new = dot_high(aug_ref[ex], jnp.concatenate([tile] * 4, axis=0)) * (1.0 / REPS)
             full[(*unit(j), my(orders[j][0]), my(orders[j][1]))] = new
+            for s in streams_of(ex):
+                if streams[s][0] == j:
+                    for d in (2, 1, 3):
+                        gather2(s, d).start()
+
+    def spread(ex):
+        for s in streams_of(ex):
+            for d in (1, 3, 2):
+                gather2(s, d).wait_recv()
             for d in (2, 1, 3):
-                gather2(j, d).start()
-
-    def spread(ex):
-        for j in (2 * ex, 2 * ex + 1):
-            for d in (1, 3, 2):
-                gather2(j, d).wait_recv()
-            for d in (2, 1, 3):
-                gather1(j, d).start()
-            forward(j, 0).start()
-
+                gather1(s, d).start()
+            forward(s, 0).start()
+
+    exchange2(0)
     for copy in gram1_copies:
         copy.wait_recv()
     total = gram1[0]
@@ -260,9 +319,10 @@
         copy.start()
         gram2_copies.append(copy)
 
-    exchange2(0)
     exchange2(1)
     exchange3(0)
+
+    exchange3(1)
 
     for copy in gram2_copies:
         copy.wait_recv()
@@ -290,35 +350,38 @@
         wanted = (lanes_at >= (2 * ex + 1) * R) & (lanes_at < (2 * ex + 2) * R)
         aug_ref[ex] = jnp.where(wanted, aug, 0.0)
 
-    exchange3(1)
     own_tile(0)
 
+    own_tile(1)
     for ex, panel in ((0, panel0), (1, panel1)):
         b = dot_high(aug_ref[ex], jnp.concatenate([panel] * 4, axis=0))
         hi, lo = [piece.astype(jnp.float32) for piece in split(b, 2)]
         basis[ex] = jnp.concatenate([hi, hi, lo, lo], axis=0).T.astype(jnp.bfloat16)
 
-    own_tile(1)
     spread(0)
     spread(1)
 
-    def finish_unit(ex, u):
+    def finish_unit(ex, u, errors):
         for p in range(SIDE):
             cols = pl.ds(pl.multiple_of(u * UNIT + p * PIECE, PIECE), PIECE)
             coeffs[ex, :, cols] = jnp.concatenate([full[ex, u, p, i] for i in range(SIDE)], axis=1)
-            if ex == 0:
+            if errors:
                 fresh[:, cols] = residual(g, e, basis, coeffs, ex, cols)
 
     for ex in range(EXP):
         for j in (2 * ex, 2 * ex + 1):
-            for d in (1, 3, 2):
-                gather1(j, d).wait_recv()
-                forward(j, SIDE - d).start()
-            finish_unit(*unit(j))
-        for j in (2 * ex, 2 * ex + 1):
-            for d in range(SIDE):
-                forward(j, d).wait_recv()
-            finish_unit(*unit_there(j))
+            for s in streams_of(ex):
+                if streams[s][0] == j:
+                    for d in (1, 3, 2):
+                        gather1(s, d).wait_recv()
+                        forward(s, SIDE - d).start()
+            finish_unit(*unit(j), ex == 0)
+    for j in range(UNITS):
+        for s in streams_of(j // 2):
+            if streams[s][0] == j:
+                for d in range(SIDE):
+                    forward(s, d).wait_recv()
+        finish_unit(*unit_there(j), j < 2)
 
     for ex in range(EXP):
         for d in (1, 2, 3):
@@ -328,9 +391,13 @@
     for j in range(UNITS):
         for d in range(SIDE):
             to_partner(j, d).wait_send()
-            forward(j, d).wait_send()
         for d in (1, 2, 3):
-            for copy in (scatter1(j, d), scatter2(j, d), scatter3(j, d), gather2(j, d), gather1(j, d)):
+            scatter3(j, d).wait_send()
+    for s in range(len(streams)):
+        for d in range(SIDE):
+            forward(s, d).wait_send()
+        for d in (1, 2, 3):
+            for copy in (scatter1(s, d), scatter2(s, d), gather2(s, d), gather1(s, d)):
                 copy.wait_send()
 
 
@@ -388,6 +455,7 @@
             pltpu.VMEM((EXP, UNITS, SIDE, R, PIECE), f32),
             pltpu.VMEM((UNITS, SIDE, R, PIECE), f32),
             pltpu.VMEM((UNITS, SIDE - 1, R, PIECE), f32),
+            pltpu.VMEM((EXP, SIDE - 1, SIDE, R // 2, TILE), f32),
             pltpu.VMEM((UNITS, SIDE, R, TILE), f32),
             pltpu.VMEM((UNITS, SIDE - 1, R, TILE), f32),
             pltpu.VMEM((UNITS, SIDE, R, TILE), f32),
@@ -396,12 +464,12 @@
             dma((EXP, 3)), dma((EXP, 3)),
             dma((7,)), dma((7,)), dma((3,)), dma((3,)),
             dma((UNITS, SIDE)), dma((UNITS, SIDE)),
+            dma((STREAMS, 3)), dma((STREAMS, 3)),
+            dma((STREAMS, 3)), dma((STREAMS, 3)),
             dma((UNITS, 3)), dma((UNITS, 3)),
-            dma((UNITS, 3)), dma((UNITS, 3)),
-            dma((UNITS, 3)), dma((UNITS, 3)),
-            dma((UNITS, 3)), dma((UNITS, 3)),
-            dma((UNITS, 3)), dma((UNITS, 3)),
-            dma((UNITS, SIDE)), dma((UNITS, SIDE)),
+            dma((STREAMS, 3)), dma((STREAMS, 3)),
+            dma((STREAMS, 3)), dma((STREAMS, 3)),
+            dma((STREAMS, SIDE)), dma((STREAMS, SIDE)),
         ],
         compiler_params=pltpu.CompilerParams(
             collective_id=0, has_side_effects=True, vmem_limit_bytes=44 * 2**20

time: 48.6 us -> 46.8 us (0.963)
  Pallas kernels: 47.9 us -> 46 us
    pallas_call x1, Pallas kernels: 44.5 us -> 42.7 us  [shards(): pl.pallas_call(kernel, out_shape=(pltpu.VMEM((ROWS, FF), b16), pltpu.VMEM...]
where the time goes in v4:
time: 46.8 us; the launch traced here: 46.7 us
  Pallas kernels  46 us (98%)
  between operations  0.64 us (1%)
    pallas_call x1, Pallas kernels, shards(): pl.pallas_call(kernel, out_shape=(pltpu.VMEM((ROWS, FF), b16), pltpu.VMEM...  42.7 us
    pallas_call x1, Pallas kernels, shards(): pl.pallas_call(store, out_shape=(jax.ShapeDtypeStruct((1, EXP, ROWS, FF),...  3.38 us

profile of v4, /device:TPU:1, one launch (start us, length us, event | category | flops | bytes accessed | tf_op | source)
XLA Modules:
  0.0 46.7 jit_solution(5358783371496239602)
XLA Ops:
  0.6 42.7 %compress.1 = (bf16[192,8192]{1,0:T(8,128)(2,1)S(1)}, f32[2,32,8192]{2,1,0:T(8,128)S(1)}, bf16[2,192,8192]{2,1,0:T(8,128)(2,1)S(1)}, bf16[2,192,8192]{2,1,0:T(8,128)(2,1)S(1)}, bf16[2,192,128]{2,1,0:T(8,128)(2,1)S(1)}) custom-call(bf16[1,2,192,8192]{3,2,1,0:T(8,128)(2,1)} %g_hbm.1, bf16[1,2,192,8192]{3,2,1,0:T(8,128)(2,1)} %e_hbm.1, f32[2,32,8192]{2,1,0:T(8,128)} %q_hbm.1), custom_call_target="tpu_custom_call" | custom-call | flops 1000000000 | bytes 25000000 | tf_op jit(solution)/shard_map/compress/pallas_call | solution.py:437
  43.3 3.4 %store.1 = (bf16[1,2,192,8192]{3,2,1,0:T(8,128)(2,1)}, f32[2,32,8192]{2,1,0:T(8,128)}) custom-call(bf16[192,8192]{1,0:T(8,128)(2,1)S(1)} %get-tuple-element.7.fresh0, f32[2,32,8192]{2,1,0:T(8,128)S(1)} %get-tuple-element.8.coeffs, bf16[2,192,8192]{2,1,0:T(8,128)(2,1)S(1)} %get-tuple-element.9.g, bf16[2,192,8192]{2,1,0:T(8,128)(2,1)S(1)} %get-tuple-element.10.e, ...), custom_call_target="tpu_custom_call" | custom-call | tf_op jit(solution)/shard_map/store/pallas_call | solution.py:480

commit v5 on v4

--- a/solution.py
+++ b/solution.py
@@ -361,28 +361,6 @@
     spread(0)
     spread(1)
 
-    def finish_unit(ex, u, errors):
-        for p in range(SIDE):
-            cols = pl.ds(pl.multiple_of(u * UNIT + p * PIECE, PIECE), PIECE)
-            coeffs[ex, :, cols] = jnp.concatenate([full[ex, u, p, i] for i in range(SIDE)], axis=1)
-            if errors:
-                fresh[:, cols] = residual(g, e, basis, coeffs, ex, cols)
-
-    for ex in range(EXP):
-        for j in (2 * ex, 2 * ex + 1):
-            for s in streams_of(ex):
-                if streams[s][0] == j:
-                    for d in (1, 3, 2):
-                        gather1(s, d).wait_recv()
-                        forward(s, SIDE - d).start()
-            finish_unit(*unit(j), ex == 0)
-    for j in range(UNITS):
-        for s in streams_of(j // 2):
-            if streams[s][0] == j:
-                for d in range(SIDE):
-                    forward(s, d).wait_recv()
-        finish_unit(*unit_there(j), j < 2)
-
     for ex in range(EXP):
         for d in (1, 2, 3):
             to_replica(ex, d).wait_send()
@@ -394,11 +372,39 @@
         for d in (1, 2, 3):
             scatter3(j, d).wait_send()
     for s in range(len(streams)):
+        for d in (1, 2, 3):
+            for copy in (scatter1(s, d), scatter2(s, d)):
+                copy.wait_send()
+
+    def finish_unit(ex, u, errors):
+        for p in range(SIDE):
+            cols = pl.ds(pl.multiple_of(u * UNIT + p * PIECE, PIECE), PIECE)
+            coeffs[ex, :, cols] = jnp.concatenate([full[ex, u, p, i] for i in range(SIDE)], axis=1)
+            if errors:
+                fresh[:, cols] = residual(g, e, basis, coeffs, ex, cols)
+
+    for ex in range(EXP):
+        for j in (2 * ex, 2 * ex + 1):
+            for s in streams_of(ex):
+                if streams[s][0] == j:
+                    for d in (1, 3, 2):
+                        gather1(s, d).wait_recv()
+                        forward(s, SIDE - d).start()
+            finish_unit(*unit(j), ex == 0)
+    for s in range(len(streams)):
+        for d in (1, 2, 3):
+            for copy in (gather2(s, d), gather1(s, d)):
+                copy.wait_send()
+    for j in range(UNITS):
+        for s in streams_of(j // 2):
+            if streams[s][0] == j:
+                for d in range(SIDE):
+                    forward(s, d).wait_recv()
+        finish_unit(*unit_there(j), j < 2)
+
+    for s in range(len(streams)):
         for d in range(SIDE):
             forward(s, d).wait_send()
-        for d in (1, 2, 3):
-            for copy in (scatter1(s, d), scatter2(s, d), gather2(s, d), gather1(s, d)):
-                copy.wait_send()
 
 
 def residual(g, e, basis, coeffs, ex, cols):

time: 46.8 us -> 46.6 us (level)
  no operation moved by 1% of the time
where the time goes in v5:
time: 46.6 us; the launch traced here: 46.5 us
  Pallas kernels  45.9 us (98%)
  between operations  0.64 us (1%)
    pallas_call x1, Pallas kernels, shards(): pl.pallas_call(kernel, out_shape=(pltpu.VMEM((ROWS, FF), b16), pltpu.VMEM...  42.5 us
    pallas_call x1, Pallas kernels, shards(): pl.pallas_call(store, out_shape=(jax.ShapeDtypeStruct((1, EXP, ROWS, FF),...  3.38 us

profile of v5, /device:TPU:1, one launch (start us, length us, event | category | flops | bytes accessed | tf_op | source)
XLA Modules:
  0.0 46.5 jit_solution(9412749397775895322)
XLA Ops:
  0.6 42.5 %compress.1 = (bf16[192,8192]{1,0:T(8,128)(2,1)S(1)}, f32[2,32,8192]{2,1,0:T(8,128)S(1)}, bf16[2,192,8192]{2,1,0:T(8,128)(2,1)S(1)}, bf16[2,192,8192]{2,1,0:T(8,128)(2,1)S(1)}, bf16[2,192,128]{2,1,0:T(8,128)(2,1)S(1)}) custom-call(bf16[1,2,192,8192]{3,2,1,0:T(8,128)(2,1)} %g_hbm.1, bf16[1,2,192,8192]{3,2,1,0:T(8,128)(2,1)} %e_hbm.1, f32[2,32,8192]{2,1,0:T(8,128)} %q_hbm.1), custom_call_target="tpu_custom_call" | custom-call | flops 1000000000 | bytes 25000000 | tf_op jit(solution)/shard_map/compress/pallas_call | solution.py:443
  43.1 3.4 %store.1 = (bf16[1,2,192,8192]{3,2,1,0:T(8,128)(2,1)}, f32[2,32,8192]{2,1,0:T(8,128)}) custom-call(bf16[192,8192]{1,0:T(8,128)(2,1)S(1)} %get-tuple-element.7.fresh0, f32[2,32,8192]{2,1,0:T(8,128)S(1)} %get-tuple-element.8.coeffs, bf16[2,192,8192]{2,1,0:T(8,128)(2,1)S(1)} %get-tuple-element.9.g, bf16[2,192,8192]{2,1,0:T(8,128)(2,1)S(1)} %get-tuple-element.10.e, ...), custom_call_target="tpu_custom_call" | custom-call | tf_op jit(solution)/shard_map/store/pallas_call | solution.py:486
